TPU v7x, 32 devices: a whole 2x2x4 slice. The times are simulated.
32 devices in a mesh: dp: 4 (over z), row: 2 (over core), col: 4 (over y, x).
Axes of the slice: x: 2, y: 2, z: 4, core: 2. Of those that a mesh axis runs over, the one named last changes fastest.
Arguments:
- features: bfloat16 [2048, 4096], P(('dp', 'row')), may hold values from -6 to 6
- w_in: bfloat16 [4096, 4096], P('row', 'col'), may hold values from -0.09375 to 0.09375
- w_out: bfloat16 [4096, 1024], P('col'), may hold values from -0.09375 to 0.09375
- captions: bfloat16 [2048, 1024], P(('dp', 'row', 'col')), may hold values from -6 to 6
- positive: int32 [2048], P(('dp', 'row')), may hold values from 0 to 2047, each once
Outputs:
- fig_terms: float32 [2048], P(('dp', 'row'))
- cap_terms: float32 [2048], P(('dp', 'row', 'col'))
- grad_w_in: float32 [4096, 4096], P(('dp', 'row'), 'col')
- grad_w_out: float32 [4096, 1024], P('col', ('dp', 'row'))
Inputs may be any that keep to these rules, and one draw needn't show every extreme that they name: positive is a permutation: every caption is the match of exactly one figure.
All inputs are finite; a program needn't handle non-finite values.
Results may differ from a plain program's by a relative error of at most 0.0053.
Values may be sent and summed in bfloat16 or wider, within the bound.
A program may use at most 128 MiB of HBM per device.

v0:
```python
import jax
import jax.numpy as jnp
from jax import lax
from jax.sharding import PartitionSpec as P

SCALE = 50.0
EPS = 1e-06


def gelu_back(pre, grad):
    return jax.vjp(jax.nn.gelu, pre)[1](grad)[0]


def on_device(features, w_in, w_out, captions, positive):
    group = ("dp", "row")
    every = ("dp", "row", "col")
    f32 = jnp.float32
    slices = lax.all_to_all(features, group, 1, 0, tiled=True)
    cap32 = captions.astype(f32)
    chat_local = (cap32 * lax.rsqrt(jnp.sum(cap32 * cap32, axis=1, keepdims=True) + EPS)).astype(
        jnp.bfloat16
    )
    chat = lax.all_gather(chat_local, every, axis=0, tiled=True)
    pre = jnp.dot(
        features, lax.all_gather(w_in, "row", axis=0, tiled=True), preferred_element_type=f32
    )
    hidden = jax.nn.gelu(pre).astype(jnp.bfloat16)
    part = jnp.dot(hidden, w_out, preferred_element_type=f32)
    emb = lax.psum_scatter(part, "col", scatter_dimension=0, tiled=True)
    mine = emb.shape[0]
    inv = lax.rsqrt(jnp.sum(emb * emb, axis=1, keepdims=True) + EPS)
    fhat = emb * inv
    fhat_b = fhat.astype(jnp.bfloat16)
    logits = SCALE * lax.dot_general(
        fhat_b, chat, (((1,), (1,)), ((), ())), preferred_element_type=f32
    )
    col = lax.axis_index("col")
    places = lax.dynamic_slice_in_dim(positive, col * mine, mine, 0)
    colids = jnp.arange(chat.shape[0], dtype=jnp.int32)
    mask = (places[:, None] == colids[None, :]).astype(f32)
    expo = jnp.exp(logits)
    picked = mask * logits
    rowsum, rowpos = (jnp.sum(expo, axis=1), jnp.sum(picked, axis=1))
    colsum, colpos = lax.psum((jnp.sum(expo, axis=0), jnp.sum(picked, axis=0)), every)
    fig_terms = lax.all_gather(jnp.log(rowsum) - rowpos, "col", axis=0, tiled=True)
    capdev = captions.shape[0]
    place = (lax.axis_index("dp") * lax.axis_size("row") + lax.axis_index("row")) * lax.axis_size(
        "col"
    ) + col
    cap_terms = lax.dynamic_slice_in_dim(jnp.log(colsum) - colpos, place * capdev, capdev, 0)
    dlog = (expo / rowsum[:, None] + expo / colsum[None, :] - 2.0 * mask).astype(jnp.bfloat16)
    dfhat = SCALE * jnp.dot(dlog, chat, preferred_element_type=f32)
    demb = ((dfhat - fhat * jnp.sum(fhat * dfhat, axis=1, keepdims=True)) * inv).astype(
        jnp.bfloat16
    )
    demb = lax.all_gather(demb, "col", axis=0, tiled=True)
    dh = lax.dot_general(demb, w_out, (((1,), (1,)), ((), ())), preferred_element_type=f32)
    dpre = gelu_back(pre, dh).astype(jnp.bfloat16)
    dpre_all = lax.all_gather(dpre, group, axis=0, tiled=True)
    head_term = lax.dot_general(hidden, demb, (((0,), (0,)), ((), ())), preferred_element_type=f32)
    grad_w_out = lax.psum_scatter(head_term, group, scatter_dimension=1, tiled=True)
    grad_w_in = lax.dot_general(
        slices, dpre_all, (((0,), (0,)), ((), ())), preferred_element_type=f32
    )
    return (fig_terms, cap_terms, grad_w_in, grad_w_out)


def solution(mesh):
    placed = (
        P(("dp", "row"), None),
        P("row", "col"),
        P("col", None),
        P(("dp", "row", "col"), None),
        P(("dp", "row")),
    )
    return jax.shard_map(
        on_device,
        mesh=mesh,
        in_specs=placed,
        out_specs=(
            P(("dp", "row")),
            P(("dp", "row", "col")),
            P(("dp", "row"), "col"),
            P("col", ("dp", "row")),
        ),
        check_vma=False,
    )
```

profile of v0, /device:TPU:0, one launch (start us, length us, event | category | flops | bytes accessed | tf_op | source)
XLA Modules:
  0.0 310.4 jit_solution(15779341503108276041)
XLA Ops:
  8.0 0.0 copy-start
  8.0 0.0 all-gather.4.cloned.1.call-start
  8.1 0.7 all-gather.4.cloned.1.call-update
  8.7 0.0 reduce-scatter.3.cloned.1.call-start
  8.8 24.2 %all-gather.4.cloned.1.call-done = bf16[4096,1024]{1,0:T(8,128)(2,1)} async-done(((bf16[2048,1024]{1,0:T(8,128)(2,1)}), bf16[4096,1024]{1,0:T(8,128)(2,1)}) %all-gather.4.cloned.1.call-update) | async-done | bytes 8388624 | tf_op jit(solution)/shard_map/all_gather | solution.py:25
  33.0 6.3 %fusion.22 = f32[256,1024]{1,0:T(8,128)S(1)} fusion(bf16[256,4096]{1,0:T(8,128)(2,1)} %param.5, bf16[4096,1024]{1,0:T(8,128)(2,1)} %all-gather.4.cloned.1.call-done), kind=kOutput, calls=%fused_computation.43 | convolution fusion | flops 2147483648 | bytes 11534336 | tf_op jit(solution)/shard_map/dot_general | solution.py:24
  39.3 0.0 copy-start.2
  39.3 1.1 copy-done.2
  40.4 0.0 copy-done
  40.4 0.0 copy-start.4
  40.4 0.0 copy-start.5
  40.4 1.8 fusion.21
  42.2 0.0 reduce-scatter.3.cloned.1.call-update
  42.2 0.0 all-gather.6.cloned.1.call-start
  42.3 0.0 copy-done.4
  42.3 0.1 fusion.10
  42.4 0.8 fusion.11
  43.2 0.0 all-gather.6.cloned.1.call-update
  43.2 0.0 all-gather.8.cloned.1.call-start
  43.3 0.0 copy-done.5
  43.3 0.1 dynamic_slice.6
  43.4 28.3 %reduce-scatter.3.cloned.1.call-done = f32[64,1024]{1,0:T(8,128)} async-done(((f32[256,1024]{1,0:T(8,128)}), f32[64,1024]{1,0:T(8,128)}) %reduce-scatter.3.cloned.1.call-update) | async-done | bytes 262160 | tf_op jit(solution)/shard_map/reduce_scatter | solution.py:29
  71.6 1.1 multiply_reduce_fusion.1
  72.7 0.0 copy-start.1
  72.7 36.8 %all-gather.6.cloned.1.call-done = bf16[2048,1024]{1,0:T(8,128)(2,1)} async-done(((bf16[64,1024]{1,0:T(8,128)(2,1)}), bf16[2048,1024]{1,0:T(8,128)(2,1)}) %all-gather.6.cloned.1.call-update) | async-done | bytes 4194320 | tf_op jit(solution)/shard_map/all_gather | solution.py:23
  109.5 3.9 %fusion.8 = (f32[2048]{0:T(1024)S(1)}, f32[64]{0:T(128)S(1)}, f32[2048]{0:T(1024)S(1)}, f32[64]{0:T(128)S(1)}, f32[64,2048]{1,0:T(8,128)S(1)}) fusion(s32[64]{0:T(128)S(1)} %dynamic_slice.6, bf16[2048,1024]{1,0:T(8,128)(2,1)} %all-gather.6.cloned.1.call-done, f32[64,1024]{1,0:T(8,128)} %reduce-scatter.3.cloned.1.call-done, f32[64]{0:T(128)S(1)} %add_rsqrt_fusion.1), kind=kOutput, calls=%fused_computation.16 | convolution fusion | flops 269479808 | bytes 4998144 | tf_op jit(solution)/shard_map/dot_general | solution.py:34
  113.4 39.3 %all-reduce.1 = (f32[2048]{0:T(1024)S(1)}, f32[2048]{0:T(1024)S(1)}) all-reduce(f32[2048]{0:T(1024)S(1)} %get-tuple-element.16, f32[2048]{0:T(1024)S(1)} %get-tuple-element.18), channel_id=1, replica_groups=mesh['dp'=4,'row'=2,'col'=4] {'dp','row','col'}, use_global_device_ids=true, to_apply=%region_8.0 | all-reduce | flops 4096 | bytes 32768 | tf_op jit(solution)/shard_map/psum | solution.py:44
  152.7 0.0 copy-done.1
  152.7 0.0 copy-start.3
  152.7 3.3 %multiply_reduce_fusion = (f32[64]{0:T(128)S(1)}, f32[64,1024]{1,0:T(8,128)S(1)}) fusion(f32[64,1024]{1,0:T(8,128)S(1)} %copy-done.1, f32[64]{0:T(128)S(1)} %add_rsqrt_fusion.1, bf16[2048,1024]{1,0:T(8,128)(2,1)} %all-gather.6.cloned.1.call-done, f32[64,2048]{1,0:T(8,128)S(1)} %get-tuple-element.22, f32[2048]{0:T(1024)S(1)} %get-tuple-element.21, ...), kind=kOutput, calls=%fused_computation.25 | convolution fusion | flops 269615040 | bytes 5252096 | tf_op jit(solution)/shard_map/dot_general | solution.py:52
  156.0 0.1 multiply_convert_fusion.1
  156.1 11.6 %all_gather.18 = bf16[256,1024]{1,0:T(8,128)(2,1)S(1)} all-gather(bf16[64,1024]{1,0:T(8,128)(2,1)S(1)} %multiply_convert_fusion.1), channel_id=1, replica_groups=mesh['dp'=4,'row'=2,'col'=4] {'col'}, dimensions={0}, use_global_device_ids=true | all-gather | bytes 655360 | tf_op jit(solution)/shard_map/all_gather | solution.py:56
  167.7 0.0 copy-done.3
  167.7 2.1 fusion.6
  169.8 0.0 all-gather.8.cloned.1.call-update
  169.8 0.0 reduce-scatter.5.cloned.1.call-start
  169.9 4.0 %fusion.20 = f32[1024,1024]{1,0:T(8,128)} fusion(bf16[256,1024]{1,0:T(8,128)(2,1)S(1)} %all_gather.18, f32[256,1024]{1,0:T(8,128)} %copy-done.2), kind=kOutput, calls=%fused_computation.41 | convolution fusion | flops 539230208 | bytes 5767168 | tf_op jit(solution)/shard_map/dot_general | solution.py:60
  173.9 0.0 reduce-scatter.5.cloned.1.call-update
  173.9 4.1 %copy.11 = bf16[256,4096]{0,1:T(8,128)(2,1)} copy(bf16[256,4096]{1,0:T(8,128)(2,1)} %param.5) | data formatting | bytes 4194304 | tf_op args[0]
  178.1 0.0 copy-start.6
  178.1 4.5 %all-to-all-start = ((bf16[256,8,512]{0,2,1:T(8,128)(2,1)}), bf16[256,8,512]{0,2,1:T(8,128)(2,1)}, u32[]{:S(2)}, u32[]{:S(2)}) async-start(bf16[256,8,512]{0,2,1:T(8,128)(2,1)} %bitcast.16), calls=%async_computation.1 | async-start | bytes 4194304 | tf_op jit(solution)/shard_map/all_to_all | solution.py:18
  182.6 0.0 copy-done.6
  182.6 0.6 dynamic-slice
  183.8 74.7 %all-to-all-done = bf16[256,8,512]{0,2,1:T(8,128)(2,1)} async-done(((bf16[256,8,512]{0,2,1:T(8,128)(2,1)}), bf16[256,8,512]{0,2,1:T(8,128)(2,1)}, u32[]{:S(2)}, u32[]{:S(2)}) %all-to-all-start) | async-done | bytes 2097184 | tf_op jit(solution)/shard_map/all_to_all | solution.py:18
  258.5 4.0 %copy.12 = bf16[8,256,512]{2,1,0:T(8,128)(2,1)} copy(bf16[8,256,512]{1,2,0:T(8,128)(2,1)} %bitcast.2) | data formatting | bytes 4194304 | tf_op jit(solution)/shard_map/all_to_all | solution.py:18
  262.5 0.1 subtract_dynamic-update-slice_fusion
  262.6 10.5 %all-reduce = f32[256]{0:T(256)} all-reduce(f32[256]{0:T(256)S(1)} %subtract_dynamic-update-slice_fusion), channel_id=1, replica_groups=mesh['dp'=4,'row'=2,'col'=4] {'col'}, use_global_device_ids=true, to_apply=%add | all-reduce | flops 256 | bytes 2048
  273.1 0.6 dynamic-slice_subtract_fusion
  273.7 0.0 all-gather.8.cloned.1.call-done
  273.7 6.7 %convolution_bitcast_fusion = f32[512,1024]{0,1:T(8,128)} fusion(bf16[2048,1024]{1,0:T(8,128)(2,1)} %all-gather.8.cloned.1.call-done, bf16[2048,512]{1,0:T(8,128)(2,1)} %bitcast.17), kind=kOutput, calls=%fused_computation.1 | convolution fusion | flops 2147483648 | bytes 8388608 | tf_op jit(solution)/shard_map/dot_general | solution.py:62
  280.4 2.9 copy.13
  283.3 19.6 %reduce-scatter.5.cloned.1.call-done = f32[1024,128]{1,0:T(8,128)} async-done(((f32[1024,1024]{1,0:T(8,128)}), f32[1024,128]{1,0:T(8,128)}) %reduce-scatter.5.cloned.1.call-update) | async-done | bytes 524304 | tf_op jit(solution)/shard_map/reduce_scatter | solution.py:61
  (3 shorter events, 0.0 us)
Async XLA Ops:
  8.0 32.4 %copy-start = (bf16[1024,1024]{1,0:T(8,128)(2,1)S(1)}, bf16[1024,1024]{1,0:T(8,128)(2,1)}, u32[]{:S(2)}) copy-start(bf16[1024,1024]{1,0:T(8,128)(2,1)} %param.7) | copy-start | bytes 6291460
  8.0 25.0 %all-gather.4.cloned.1.call-start = ((), (), s32[]{:S(2)}) async-start(), calls=%async_computation.3 | async-start | bytes 12582912 | tf_op jit(solution)/shard_map/all_gather | solution.py:25
  8.7 62.9 %reduce-scatter.3.cloned.1.call-start = ((), (), s32[]{:S(2)}) async-start(), calls=%async_computation.4 | async-start | bytes 1310720 | tf_op jit(solution)/shard_map/reduce_scatter | solution.py:29
  39.3 1.1 copy-start.2
  40.4 1.9 copy-start.4
  40.4 2.9 copy-start.5
  42.2 67.3 %all-gather.6.cloned.1.call-start = ((), (), s32[]{:S(2)}) async-start(), calls=%async_computation.5 | async-start | bytes 4325376 | tf_op jit(solution)/shard_map/all_gather | solution.py:23
  43.2 230.5 %all-gather.8.cloned.1.call-start = ((), (), s32[]{:S(2)}) async-start(), calls=%async_computation.6 | async-start | bytes 4718592 | tf_op jit(solution)/shard_map/all_gather | solution.py:59
  72.7 80.0 %copy-start.1 = (f32[64,1024]{1,0:T(8,128)S(1)}, f32[64,1024]{1,0:T(8,128)}, u32[]{:S(2)}) copy-start(f32[64,1024]{1,0:T(8,128)} %reduce-scatter.3.cloned.1.call-done) | copy-start | bytes 786436
  152.7 15.0 %copy-start.3 = (f32[256,1024]{1,0:T(8,128)S(1)}, f32[256,1024]{1,0:T(8,128)}, u32[]{:S(2)}) copy-start(f32[256,1024]{1,0:T(8,128)} %copy-done.2) | copy-start | bytes 3145732
  169.8 133.0 %reduce-scatter.5.cloned.1.call-start = ((), (), s32[]{:S(2)}) async-start(), calls=%async_computation.7 | async-start | bytes 4718592 | tf_op jit(solution)/shard_map/reduce_scatter | solution.py:61
  178.1 4.5 %copy-start.6 = (u32[32]{0:T(128)S(1)}, u32[32]{0:T(128)}, u32[]{:S(2)}) copy-start(u32[32]{0:T(128)} %constant.49) | copy-start | bytes 388
  178.1 80.4 %all-to-all-start = ((bf16[256,8,512]{0,2,1:T(8,128)(2,1)}), bf16[256,8,512]{0,2,1:T(8,128)(2,1)}, u32[]{:S(2)}, u32[]{:S(2)}) async-start(bf16[256,8,512]{0,2,1:T(8,128)(2,1)} %bitcast.16), calls=%async_computation.1 | async-start | bytes 4194304 | tf_op jit(solution)/shard_map/all_to_all | solution.py:18
Sparse Core Ops, SparseCore 0:
  10.4 22.5 all-gather.3
  42.4 29.2 reduce-scatter.2
Sparse Core Ops, SparseCore 1:
  46.2 63.3 all-gather.5
  169.9 81.1 all-gather.7
  253.9 48.9 reduce-scatter.4
where the time goes:
time: 311 us; the launch traced here: 310 us
  waiting for transfers between devices  184 us (59%)
  blocking collectives  61.4 us (20%)
  matrix products  28.1 us (9%)
  between operations  16.4 us (5%)
  local copies, waits for them, and re-layouts  12.8 us (4%)
  starting transfers between devices  4.7 us (2%)
    all_to_all x1, waiting for transfers between devices, on_device(): slices = lax.all_to_all(features, group, 1, 0, tiled=True)  74.7 us
    psum x1, blocking collectives, on_device(): lax.psum((jnp.sum(expo, axis=0), jnp.sum(picked, axis=0)), every)  39.3 us
    all_gather x1, waiting for transfers between devices, on_device(): chat = lax.all_gather(chat_local, every, axis=0, tiled=True)  36.8 us
    reduce_scatter x1, waiting for transfers between devices, on_device(): emb = lax.psum_scatter(part, 'col', scatter_dimension=0, tiled=True)  28.3 us
    all_gather x1, waiting for transfers between devices, on_device(): lax.all_gather(w_in, 'row', axis=0, tiled=True)  24.2 us
    reduce_scatter x1, waiting for transfers between devices, on_device(): lax.psum_scatter(head_term, group, scatter_dimension=1, tiled=True)  19.6 us
    all_gather x1, blocking collectives, on_device(): demb = lax.all_gather(demb, 'col', axis=0, tiled=True)  11.6 us
    unnamed x1, blocking collectives  10.5 us
  transfers between devices with their start and end apart: 6, of which 5 were waited for; matrix products, arithmetic and copies ran while one was open for 8% of the time, Pallas kernels for 0%

commit v1 on v0

--- a/solution.py
+++ b/solution.py
@@ -5,6 +5,18 @@
 
 SCALE = 50.0
 EPS = 1e-06
+
+
+def collect(array, axis, dim):
+    ways, here, step = (lax.axis_size(axis), lax.axis_index(axis), array.shape[dim])
+    shape = [n * ways if d == dim else n for d, n in enumerate(array.shape)]
+    full = lax.dynamic_update_slice_in_dim(
+        jnp.zeros(shape, array.dtype), array, here * step, axis=dim
+    )
+    for far in range(1, ways):
+        array = lax.ppermute(array, axis, [(d, (d + 1) % ways) for d in range(ways)])
+        full = lax.dynamic_update_slice_in_dim(full, array, (here - far) % ways * step, axis=dim)
+    return full
 
 
 def gelu_back(pre, grad):
@@ -53,7 +65,7 @@
     demb = ((dfhat - fhat * jnp.sum(fhat * dfhat, axis=1, keepdims=True)) * inv).astype(
         jnp.bfloat16
     )
-    demb = lax.all_gather(demb, "col", axis=0, tiled=True)
+    demb = collect(demb, "col", 0)
     dh = lax.dot_general(demb, w_out, (((1,), (1,)), ((), ())), preferred_element_type=f32)
     dpre = gelu_back(pre, dh).astype(jnp.bfloat16)
     dpre_all = lax.all_gather(dpre, group, axis=0, tiled=True)

time: 311 us -> 320 us (1.029)
  waiting for transfers between devices: 184 us -> 200 us
  blocking collectives: 61.4 us -> 49.7 us
  starting transfers between devices: 4.7 us -> 8.42 us
    ppermute x0 -> x3, waiting for transfers between devices: none -> 14.4 us  [collect(): lax.ppermute(array, axis, [(d, (d + 1) % ways) for d in range(ways)])]
    all_gather x1 -> x0, blocking collectives: 11.6 us -> none  [on_device(): demb = lax.all_gather(demb, 'col', axis=0, tiled=True)]
    ppermute x0 -> x3, starting transfers between devices: none -> 3.73 us  [collect(): lax.ppermute(array, axis, [(d, (d + 1) % ways) for d in range(ways)])]
    unnamed x18 -> x16, local copies, waits for them, and re-layouts: 8.7 us -> 8.71 us
  transfers between devices with their start and end apart: 6 -> 9, of which waited for: 5 -> 8; matrix products, arithmetic and copies ran while one was open for 8% -> 8% of each run, Pallas kernels for 0% -> 0%
where the time goes in v1:
time: 320 us; the launch traced here: 319 us
  waiting for transfers between devices  200 us (62%)
  blocking collectives  49.7 us (16%)
  matrix products  29.2 us (9%)
  between operations  16.5 us (5%)
  local copies, waits for them, and re-layouts  12.8 us (4%)
  starting transfers between devices  8.42 us (3%)
    all_to_all x1, waiting for transfers between devices, on_device(): slices = lax.all_to_all(features, group, 1, 0, tiled=True)  75 us
    psum x1, blocking collectives, on_device(): lax.psum((jnp.sum(expo, axis=0), jnp.sum(picked, axis=0)), every)  39.3 us
    all_gather x1, waiting for transfers between devices, on_device(): chat = lax.all_gather(chat_local, every, axis=0, tiled=True)  36.8 us
    reduce_scatter x1, waiting for transfers between devices, on_device(): emb = lax.psum_scatter(part, 'col', scatter_dimension=0, tiled=True)  28.3 us
    all_gather x1, waiting for transfers between devices, on_device(): lax.all_gather(w_in, 'row', axis=0, tiled=True)  24.2 us
    reduce_scatter x1, waiting for transfers between devices, on_device(): lax.psum_scatter(head_term, group, scatter_dimension=1, tiled=True)  20.7 us
    ppermute x3, waiting for transfers between devices, collect(): lax.ppermute(array, axis, [(d, (d + 1) % ways) for d in range(ways)])  14.4 us
    unnamed x1, blocking collectives  10.4 us
  transfers between devices with their start and end apart: 9, of which 8 were waited for; matrix products, arithmetic and copies ran while one was open for 8% of the time, Pallas kernels for 0%

profile of v1, /device:TPU:0, one launch (start us, length us, event | category | flops | bytes accessed | tf_op | source)
XLA Modules:
  0.0 319.5 jit_solution(2114215066944833400)
XLA Ops:
  8.0 0.0 copy-start
  8.0 0.0 all-gather.4.cloned.1.call-start
  8.1 0.7 all-gather.4.cloned.1.call-update
  8.7 0.0 reduce-scatter.3.cloned.1.call-start
  8.8 24.2 %all-gather.4.cloned.1.call-done = bf16[4096,1024]{1,0:T(8,128)(2,1)} async-done(((bf16[2048,1024]{1,0:T(8,128)(2,1)}), bf16[4096,1024]{1,0:T(8,128)(2,1)}) %all-gather.4.cloned.1.call-update) | async-done | bytes 8388624 | tf_op jit(solution)/shard_map/all_gather | solution.py:37
  33.0 6.3 %fusion.22 = f32[256,1024]{1,0:T(8,128)S(1)} fusion(bf16[256,4096]{1,0:T(8,128)(2,1)} %param.5, bf16[4096,1024]{1,0:T(8,128)(2,1)} %all-gather.4.cloned.1.call-done), kind=kOutput, calls=%fused_computation.47 | convolution fusion | flops 2147483648 | bytes 11534336 | tf_op jit(solution)/shard_map/dot_general | solution.py:36
  39.3 0.0 copy-start.2
  39.3 1.1 copy-done.2
  40.4 0.0 copy-done
  40.4 0.0 copy-start.3
  40.4 0.0 copy-start.4
  40.4 1.8 fusion.21
  42.2 0.0 reduce-scatter.3.cloned.1.call-update
  42.2 0.0 all-gather.6.cloned.1.call-start
  42.3 0.0 copy-done.3
  42.3 0.1 fusion.10
  42.4 0.8 fusion.11
  43.2 0.0 all-gather.6.cloned.1.call-update
  43.2 0.0 all-gather.8.cloned.1.call-start
  43.3 0.0 copy-done.4
  43.3 0.1 dynamic_slice.6
  43.4 28.3 %reduce-scatter.3.cloned.1.call-done = f32[64,1024]{1,0:T(8,128)} async-done(((f32[256,1024]{1,0:T(8,128)}), f32[64,1024]{1,0:T(8,128)}) %reduce-scatter.3.cloned.1.call-update) | async-done | bytes 262160 | tf_op jit(solution)/shard_map/reduce_scatter | solution.py:41
  71.6 1.1 multiply_reduce_fusion.1
  72.7 0.0 copy-start.1
  72.7 36.8 %all-gather.6.cloned.1.call-done = bf16[2048,1024]{1,0:T(8,128)(2,1)} async-done(((bf16[64,1024]{1,0:T(8,128)(2,1)}), bf16[2048,1024]{1,0:T(8,128)(2,1)}) %all-gather.6.cloned.1.call-update) | async-done | bytes 4194320 | tf_op jit(solution)/shard_map/all_gather | solution.py:35
  109.5 3.9 %fusion.8 = (f32[2048]{0:T(1024)S(1)}, f32[64]{0:T(128)S(1)}, f32[2048]{0:T(1024)S(1)}, f32[64]{0:T(128)S(1)}, f32[64,2048]{1,0:T(8,128)S(1)}) fusion(s32[64]{0:T(128)S(1)} %dynamic_slice.6, bf16[2048,1024]{1,0:T(8,128)(2,1)} %all-gather.6.cloned.1.call-done, f32[64,1024]{1,0:T(8,128)} %reduce-scatter.3.cloned.1.call-done, f32[64]{0:T(128)S(1)} %add_rsqrt_fusion.1), kind=kOutput, calls=%fused_computation.16 | convolution fusion | flops 269479808 | bytes 4998144 | tf_op jit(solution)/shard_map/dot_general | solution.py:46
  113.4 39.3 %all-reduce.1 = (f32[2048]{0:T(1024)S(1)}, f32[2048]{0:T(1024)S(1)}) all-reduce(f32[2048]{0:T(1024)S(1)} %get-tuple-element.16, f32[2048]{0:T(1024)S(1)} %get-tuple-element.18), channel_id=1, replica_groups=mesh['dp'=4,'row'=2,'col'=4] {'dp','row','col'}, use_global_device_ids=true, to_apply=%region_8.0 | all-reduce | flops 4096 | bytes 32768 | tf_op jit(solution)/shard_map/psum | solution.py:56
  152.7 0.0 copy-done.1
  152.7 3.2 %multiply_reduce_fusion = (f32[64]{0:T(128)S(1)}, f32[64,1024]{1,0:T(8,128)S(1)}) fusion(f32[64,1024]{1,0:T(8,128)S(1)} %copy-done.1, f32[64]{0:T(128)S(1)} %add_rsqrt_fusion.1, bf16[2048,1024]{1,0:T(8,128)(2,1)} %all-gather.6.cloned.1.call-done, f32[64,2048]{1,0:T(8,128)S(1)} %get-tuple-element.24, f32[2048]{0:T(1024)S(1)} %get-tuple-element.21, ...), kind=kOutput, calls=%fused_computation.25 | convolution fusion | flops 269615040 | bytes 5252096 | tf_op jit(solution)/shard_map/dot_general | solution.py:64
  155.9 0.1 broadcast_in_dim.2
  156.0 0.1 constant_dynamic-update-slice_fusion.3
  156.1 2.3 collective-permute-start
  158.4 4.0 %collective-permute-done = bf16[64,1024]{1,0:T(8,128)(2,1)S(1)} collective-permute-done((bf16[64,1024]{1,0:T(8,128)(2,1)S(1)}, bf16[64,1024]{1,0:T(8,128)(2,1)S(1)}, u32[]{:S(2)}, u32[]{:S(2)}) %collective-permute-start) | collective-permute-done | bytes 131104 | tf_op jit(solution)/shard_map/ppermute | solution.py:17
  162.4 1.0 collective-permute-start.1
  163.4 5.0 %collective-permute-done.1 = bf16[64,1024]{1,0:T(8,128)(2,1)S(1)} collective-permute-done((bf16[64,1024]{1,0:T(8,128)(2,1)S(1)}, bf16[64,1024]{1,0:T(8,128)(2,1)S(1)}, u32[]{:S(2)}, u32[]{:S(2)}) %collective-permute-start.1) | collective-permute-done | bytes 131104 | tf_op jit(solution)/shard_map/ppermute | solution.py:17
  168.4 0.4 collective-permute-start.2
  168.8 5.4 %collective-permute-done.2 = bf16[64,1024]{1,0:T(8,128)(2,1)S(1)} collective-permute-done((bf16[64,1024]{1,0:T(8,128)(2,1)S(1)}, bf16[64,1024]{1,0:T(8,128)(2,1)S(1)}, u32[]{:S(2)}, u32[]{:S(2)}) %collective-permute-start.2) | collective-permute-done | bytes 131104 | tf_op jit(solution)/shard_map/ppermute | solution.py:17
  174.3 3.3 %fusion.6 = bf16[256,1024]{1,0:T(8,128)(2,1)} fusion(f32[256,1024]{1,0:T(8,128)} %copy-done.2, bf16[256,1024]{1,0:T(8,128)(2,1)S(1)} %constant_dynamic-update-slice_fusion, bf16[1024,1024]{1,0:T(8,128)(2,1)S(1)} %copy-done), kind=kOutput, calls=%fused_computation.11 | convolution fusion | flops 542113792 | bytes 4194304 | tf_op jit(solution)/shard_map/dot_general | solution.py:69
  177.5 0.0 all-gather.8.cloned.1.call-update
  177.6 0.0 reduce-scatter.5.cloned.1.call-start
  177.6 4.0 %fusion.20 = f32[1024,1024]{1,0:T(8,128)} fusion(bf16[256,1024]{1,0:T(8,128)(2,1)S(1)} %constant_dynamic-update-slice_fusion, f32[256,1024]{1,0:T(8,128)} %copy-done.2), kind=kOutput, calls=%fused_computation.45 | convolution fusion | flops 539230208 | bytes 5767168 | tf_op jit(solution)/shard_map/dot_general | solution.py:72
  181.7 0.0 reduce-scatter.5.cloned.1.call-update
  181.7 4.2 %copy.11 = bf16[256,4096]{0,1:T(8,128)(2,1)} copy(bf16[256,4096]{1,0:T(8,128)(2,1)} %param.5) | data formatting | bytes 4194304 | tf_op args[0]
  185.8 0.0 copy-start.5
  185.8 4.5 %all-to-all-start = ((bf16[256,8,512]{0,2,1:T(8,128)(2,1)}), bf16[256,8,512]{0,2,1:T(8,128)(2,1)}, u32[]{:S(2)}, u32[]{:S(2)}) async-start(bf16[256,8,512]{0,2,1:T(8,128)(2,1)} %bitcast.16), calls=%async_computation.1 | async-start | bytes 4194304 | tf_op jit(solution)/shard_map/all_to_all | solution.py:30
  190.3 0.0 copy-done.5
  190.4 0.6 dynamic-slice
  191.6 75.0 %all-to-all-done = bf16[256,8,512]{0,2,1:T(8,128)(2,1)} async-done(((bf16[256,8,512]{0,2,1:T(8,128)(2,1)}), bf16[256,8,512]{0,2,1:T(8,128)(2,1)}, u32[]{:S(2)}, u32[]{:S(2)}) %all-to-all-start) | async-done | bytes 2097184 | tf_op jit(solution)/shard_map/all_to_all | solution.py:30
  266.6 3.9 %copy.12 = bf16[8,256,512]{2,1,0:T(8,128)(2,1)} copy(bf16[8,256,512]{1,2,0:T(8,128)(2,1)} %bitcast.2) | data formatting | bytes 4194304 | tf_op jit(solution)/shard_map/all_to_all | solution.py:30
  270.5 0.1 subtract_dynamic-update-slice_fusion
  270.6 10.4 %all-reduce = f32[256]{0:T(256)} all-reduce(f32[256]{0:T(256)S(1)} %subtract_dynamic-update-slice_fusion), channel_id=1, replica_groups=mesh['dp'=4,'row'=2,'col'=4] {'col'}, use_global_device_ids=true, to_apply=%add | all-reduce | flops 256 | bytes 2048
  281.0 0.6 dynamic-slice_subtract_fusion
  281.6 0.0 all-gather.8.cloned.1.call-done
  281.6 6.7 %convolution_bitcast_fusion = f32[512,1024]{0,1:T(8,128)} fusion(bf16[2048,1024]{1,0:T(8,128)(2,1)} %all-gather.8.cloned.1.call-done, bf16[2048,512]{1,0:T(8,128)(2,1)} %bitcast.17), kind=kOutput, calls=%fused_computation.1 | convolution fusion | flops 2147483648 | bytes 8388608 | tf_op jit(solution)/shard_map/dot_general | solution.py:74
  288.3 2.9 copy.13
  291.2 20.7 %reduce-scatter.5.cloned.1.call-done = f32[1024,128]{1,0:T(8,128)} async-done(((f32[1024,1024]{1,0:T(8,128)}), f32[1024,128]{1,0:T(8,128)}) %reduce-scatter.5.cloned.1.call-update) | async-done | bytes 524304 | tf_op jit(solution)/shard_map/reduce_scatter | solution.py:73
  (6 shorter events, 0.1 us)
Async XLA Ops:
  8.0 32.4 %copy-start = (bf16[1024,1024]{1,0:T(8,128)(2,1)S(1)}, bf16[1024,1024]{1,0:T(8,128)(2,1)}, u32[]{:S(2)}) copy-start(bf16[1024,1024]{1,0:T(8,128)(2,1)} %param.7) | copy-start | bytes 6291460
  8.0 25.0 %all-gather.4.cloned.1.call-start = ((), (), s32[]{:S(2)}) async-start(), calls=%async_computation.3 | async-start | bytes 12582912 | tf_op jit(solution)/shard_map/all_gather | solution.py:37
  8.7 62.9 %reduce-scatter.3.cloned.1.call-start = ((), (), s32[]{:S(2)}) async-start(), calls=%async_computation.4 | async-start | bytes 1310720 | tf_op jit(solution)/shard_map/reduce_scatter | solution.py:41
  39.3 1.1 copy-start.2
  40.4 1.9 copy-start.3
  40.4 2.9 copy-start.4
  42.2 67.3 %all-gather.6.cloned.1.call-start = ((), (), s32[]{:S(2)}) async-start(), calls=%async_computation.5 | async-start | bytes 4325376 | tf_op jit(solution)/shard_map/all_gather | solution.py:35
  43.2 238.4 %all-gather.8.cloned.1.call-start = ((), (), s32[]{:S(2)}) async-start(), calls=%async_computation.6 | async-start | bytes 4718592 | tf_op jit(solution)/shard_map/all_gather | solution.py:71
  72.7 80.0 %copy-start.1 = (f32[64,1024]{1,0:T(8,128)S(1)}, f32[64,1024]{1,0:T(8,128)}, u32[]{:S(2)}) copy-start(f32[64,1024]{1,0:T(8,128)} %reduce-scatter.3.cloned.1.call-done) | copy-start | bytes 786436
  156.1 6.3 %collective-permute-start = (bf16[64,1024]{1,0:T(8,128)(2,1)S(1)}, bf16[64,1024]{1,0:T(8,128)(2,1)S(1)}, u32[]{:S(2)}, u32[]{:S(2)}) collective-permute-start(bf16[64,1024]{1,0:T(8,128)(2,1)S(1)} %get-tuple-element.23), channel_id=1, source_target_pairs={{0,1},{1,2},{2,3},{3,0},{4,5},{5,6},{6,7},{7,4},{8,9},{9,10},{10,1... | collective-permute-start | bytes 393224 | tf_op jit(solution)/shard_map/ppermute | solution.py:17
  162.4 6.0 %collective-permute-start.1 = (bf16[64,1024]{1,0:T(8,128)(2,1)S(1)}, bf16[64,1024]{1,0:T(8,128)(2,1)S(1)}, u32[]{:S(2)}, u32[]{:S(2)}) collective-permute-start(bf16[64,1024]{1,0:T(8,128)(2,1)S(1)} %collective-permute-done), channel_id=1, source_target_pairs={{0,1},{1,2},{2,3},{3,0},{4,5},{5,6},{6,7},{7,4},{8,9},{9,10},{10,1... | collective-permute-start | bytes 393224 | tf_op jit(solution)/shard_map/ppermute | solution.py:17
  168.4 5.9 %collective-permute-start.2 = (bf16[64,1024]{1,0:T(8,128)(2,1)S(1)}, bf16[64,1024]{1,0:T(8,128)(2,1)S(1)}, u32[]{:S(2)}, u32[]{:S(2)}) collective-permute-start(bf16[64,1024]{1,0:T(8,128)(2,1)S(1)} %collective-permute-done.1), channel_id=1, source_target_pairs={{0,1},{1,2},{2,3},{3,0},{4,5},{5,6},{6,7},{7,4},{8,9},{9,10},{10,1... | collective-permute-start | bytes 393224 | tf_op jit(solution)/shard_map/ppermute | solution.py:17
  177.6 134.4 %reduce-scatter.5.cloned.1.call-start = ((), (), s32[]{:S(2)}) async-start(), calls=%async_computation.7 | async-start | bytes 4718592 | tf_op jit(solution)/shard_map/reduce_scatter | solution.py:73
  185.8 4.5 %copy-start.5 = (u32[32]{0:T(128)S(1)}, u32[32]{0:T(128)}, u32[]{:S(2)}) copy-start(u32[32]{0:T(128)} %constant.77) | copy-start | bytes 388
  185.8 80.8 %all-to-all-start = ((bf16[256,8,512]{0,2,1:T(8,128)(2,1)}), bf16[256,8,512]{0,2,1:T(8,128)(2,1)}, u32[]{:S(2)}, u32[]{:S(2)}) async-start(bf16[256,8,512]{0,2,1:T(8,128)(2,1)} %bitcast.16), calls=%async_computation.1 | async-start | bytes 4194304 | tf_op jit(solution)/shard_map/all_to_all | solution.py:30
Sparse Core Ops, SparseCore 0:
  10.4 22.5 all-gather.3
  42.4 29.2 reduce-scatter.2
Sparse Core Ops, SparseCore 1:
  46.2 63.3 all-gather.5
  177.6 81.6 all-gather.7
  262.1 49.7 reduce-scatter.4
